TPU v7x, 32 devices: a whole 2x2x4 slice. The times are simulated.
32 devices in a mesh: peel: 2 (over x), tile: 16 (over z, y, core).
Axes of the slice: x: 2, y: 2, z: 4, core: 2. Of those that a mesh axis runs over, the one named last changes fastest.
Arguments:
- season_ids: int32 [16], P('peel'), parts along dimension 0, may hold values from 0 to 23
- season_table: float32 [5, 24], replicated, may hold values from 0.5 to 2
- shelf_mask: int32 [128, 1024], P('tile'), may hold values 0 or 1
- codes: int32 [128, 1024], P('tile'), may hold values from 0 to 3
- spawn: float32 [128, 1024], P('tile'), may hold values from 0.2 to 5
- survey: float32 [4, 128, 1024], P('peel', 'tile'), parts along dimension 0, may hold values from 0.2 to 2
Outputs:
- concentration: float32 [16, 128, 1024], P('peel', 'tile'), parts along dimension 0
- adjoint: float32 [16, 128, 1024], P('peel', 'tile'), parts along dimension 0
- gradient: float32 [128, 2048], P('tile', 'peel'), parts along dimension 1
There are 2 independent parts, one for each index of `peel`. A program takes and returns all parts, laid end to end along the dimension named above; an argument that names none is the same for every part. Nothing has to cross between parts.
Inputs may be any that keep to these rules, and one draw needn't show every extreme that they name: `season_ids`: seasons may repeat within a peel. `codes`: bit 0 of a code picks the upwind neighbour along the first dimension (0: the lower index), bit 1 along the second.
All inputs are finite; a program needn't handle non-finite values. No bound on the sum of `shelf_mask` on one device may be relied on, other than what follows from the above.
Results may differ from a plain program's by a relative error of at most 0.0003.
Values sent between devices are 32-bit elements; how exact they have to be, the bound alone decides.
A program may use at most 64 MiB of HBM per device.

v0:
```python
import functools

import jax
import jax.numpy as jnp
from jax import lax
from jax.experimental import pallas as pl
from jax.experimental.pallas import tpu as pltpu
from jax.sharding import PartitionSpec as P


f32, bf16 = jnp.float32, jnp.bfloat16
REACH = 8
STRIP = 8
HALO = 6


def wide(p, width):
    return jnp.concatenate([p] * (width // 128), axis=1) if width > 128 else p


def kernel(n, ny, prm, mask, codes, spawn, survey, c_out, a_out, g_out,
           strips, tgt, s0, west, south, f0, cn, cs, cw, ce, f1, it, up, dl,
           s1, k1, b1, u1, v1, s2, k2, b2, u2, s3own, b3own, win,
           send_n, recv_n, send_g, recv_g):
    me = lax.axis_index("tile")
    n1, n2, n3 = ny // 2, ny // 4, ny // 8

    def guarded(d, body):
        ok = (me + d >= 0) & (me + d < n)
        pl.when(ok)(body)

    strips[...] = jnp.zeros_like(strips)
    tgt[...] = jnp.zeros_like(tgt)
    f1[...] = jnp.zeros_like(f1)
    b2[...] = jnp.zeros_like(b2)
    win[...] = jnp.zeros_like(win)
    strips[0, STRIP:2 * STRIP, :] = jnp.where(mask[...] > 0, 1.0, 0.0).astype(f32)
    strips[1, STRIP:2 * STRIP, :] = codes[...].astype(f32)
    strips[2, STRIP:2 * STRIP, :] = spawn[...]
    barrier = pltpu.get_barrier_semaphore()
    offsets = [d for k in range(1, REACH + 1) for d in (-k, k)]
    for d in offsets:
        guarded(d, lambda d=d: pl.semaphore_signal(
            barrier, inc=1, device_id={"tile": me + d}, device_id_type=pl.DeviceIdType.MESH))
    pl.semaphore_wait(barrier, jnp.minimum(me, REACH) + jnp.minimum(n - 1 - me, REACH))

    def copy(src, dst, ssem, rsem, d):
        return pltpu.make_async_remote_copy(
            src_ref=src, dst_ref=dst, send_sem=ssem, recv_sem=rsem,
            device_id={"tile": me + d}, device_id_type=pl.DeviceIdType.MESH)

    def swap(k, up_src, up_dst, down_src, down_dst):
        def at(d):
            side = 0 if d < 0 else 1
            src, dst = (up_src, up_dst) if d < 0 else (down_src, down_dst)
            return copy(src, dst, send_n.at[k, side], recv_n.at[k, side], d)
        for d in (-1, 1):
            guarded(d, lambda d=d: at(d).start())
        guarded(1, lambda: copy(up_src, up_dst, send_n.at[k, 0], recv_n.at[k, 0], 1).wait_recv())
        guarded(-1, lambda: copy(down_src, down_dst, send_n.at[k, 1], recv_n.at[k, 1], -1).wait_recv())
        for d in (-1, 1):
            guarded(d, lambda d=d: at(d).wait_send())

    def gather_start(k, src):
        for d in offsets:
            guarded(d, lambda d=d: copy(src, win.at[k, REACH - d], send_g.at[k, REACH - d],
                                        recv_g.at[k, REACH - d], d).start())

    def gather_wait(k, src):
        for d in offsets:
            guarded(d, lambda d=d: copy(src, win.at[k, REACH + d], send_g.at[k, REACH + d],
                                        recv_g.at[k, REACH + d], d).wait_recv())
        for d in offsets:
            guarded(d, lambda d=d: copy(src, win.at[k, REACH - d], send_g.at[k, REACH - d],
                                        recv_g.at[k, REACH - d], d).wait_send())

    swap(0, strips.at[:, 8:16], strips.at[:, 16:24], strips.at[:, 8:16], strips.at[:, 0:8])

    gi = lax.broadcasted_iota(jnp.int32, (256, 128), 0)
    gj = lax.broadcasted_iota(jnp.int32, (256, 128), 1)
    pair_sum = jnp.where(gi // 2 == gj, 1.0, 0.0).astype(bf16)
    hi_ = lax.broadcasted_iota(jnp.int32, (128, 256), 0)
    hj_ = lax.broadcasted_iota(jnp.int32, (128, 256), 1)
    spread = jnp.where(hj_ // 2 == hi_, 1.0, 0.0).astype(bf16)

    def times(x, m):
        big = x.astype(bf16)
        rest = (x - big.astype(f32)).astype(bf16)
        return (jnp.dot(big, m, preferred_element_type=f32)
                + jnp.dot(rest, m, preferred_element_type=f32))

    def restrict(src, lo, count, width):
        blocks = width // 256
        stack = []
        for i in range(count):
            x = src[lo + 2 * i] + src[lo + 2 * i + 1]
            stack += [x[:, b * 256:(b + 1) * 256] for b in range(blocks)]
        y = times(jnp.concatenate(stack, axis=0), pair_sum)
        rows = []
        for i in range(count):
            parts = [y[(i * blocks + b) * 8:(i * blocks + b + 1) * 8] for b in range(blocks)]
            rows.append(jnp.concatenate(parts, axis=1) if blocks > 1 else parts[0])
        return rows

    def prolong(rows):
        blocks = rows[0].shape[1] // 128
        stack = [x[:, b * 128:(b + 1) * 128] for x in rows for b in range(blocks)]
        y = times(jnp.concatenate(stack, axis=0), spread)
        out = []
        for i in range(len(rows)):
            parts = [y[(i * blocks + b) * 8:(i * blocks + b + 1) * 8] for b in range(blocks)]
            out.append(jnp.concatenate(parts, axis=1) if blocks > 1 else parts[0])
        return out

    def lanes(width):
        return lax.broadcasted_iota(jnp.int32, (8, width), 1)

    def shifted(x):
        width = x.shape[1]
        lane = lanes(width)
        return (jnp.where(lane == 0, 0.0, pltpu.roll(x, 1, 1)),
                jnp.where(lane == width - 1, 0.0, pltpu.roll(x, width - 1, 1)))

    g0, dd, uu, vv, strength = prm[0], prm[1], prm[2], prm[3], prm[4]
    kappa = [None, prm[5], prm[6], prm[7]]
    ratio = [prm[8], prm[9], prm[10]]

    for r in range(24):
        s0[r] = jnp.broadcast_to(strips[0, r:r + 1, :], (8, ny))
        code = strips[1, r:r + 1, :]
        top = jnp.where(code >= 2.0, 1.0, 0.0)
        west[r] = jnp.broadcast_to(1.0 - (code - 2.0 * top), (8, ny))
        south[r] = jnp.broadcast_to(1.0 - top, (8, ny))
        f0[r] = s0[r] * wide(g0 * strength, ny) * jnp.broadcast_to(strips[2, r:r + 1, :], (8, ny))
    for i, x in enumerate(restrict(s0, 0, 12, ny)):
        s1[i] = jnp.where(x > 0.0, 1.0, 0.0)
        k1[i] = s1[i] * wide(kappa[1], n1)
    for i, x in enumerate(restrict(s1, 0, 6, n1)):
        s2[i] = jnp.where(x > 0.0, 1.0, 0.0)
        k2[i] = s2[i] * wide(kappa[2], n2)
    own3 = restrict(s2, 2, 1, n2)[0]
    s3own[...] = jnp.where(own3 > 0.0, 1.0, 0.0)
    gather_start(0, s3own)

    def loop(lo, hi, body):
        lax.fori_loop(lo, hi, lambda r, c: (body(r), c)[1], 0)

    def coefficients(adjoint):
        D = wide(dd, ny)
        U = wide(uu, ny)
        V = wide(vv, ny)

        def row(r):
            lane = lanes(ny)
            s = s0[r]
            if adjoint:
                an, as_ = 1.0 - west[r - 1], west[r + 1]
                so = south[r]
                bw, be = 1.0 - pltpu.roll(so, 1, 1), pltpu.roll(so, ny - 1, 1)
            else:
                an, bw = west[r], south[r]
                as_, be = 1.0 - an, 1.0 - bw
            cn[r] = s * (D + U * an)
            cs[r] = s * (D + U * as_)
            cw[r] = jnp.where(lane == 0, 0.0, s * (D + V * bw))
            ce[r] = jnp.where(lane == ny - 1, 0.0, s * (D + V * be))
        loop(3, 21, row)

    def relaxed0(f, r):
        x = f[r]
        return (0.2 * x + f0[r] + (cn[r] * f[r - 1] + cs[r] * f[r + 1])
                + (cw[r] * pltpu.roll(x, 1, 1) + ce[r] * pltpu.roll(x, ny - 1, 1)))

    def relaxed(f, b, k, r):
        x = f[r]
        w, e = shifted(x)
        return 0.2 * x + b[r] + k[r] * ((f[r - 1] + f[r + 1]) + (w + e))

    def coarse(k, s3):
        src = win[k]
        b = jnp.concatenate([src[i] for i in range(2 * REACH + 1)], axis=0)
        weight = jnp.concatenate([s3[i] * kappa[3] for i in range(2 * REACH + 1)], axis=0)
        lane = lax.broadcasted_iota(jnp.int32, b.shape, 1)
        left = jnp.where(lane == 0, 0.0, weight)
        right = jnp.where(lane == n3 - 1, 0.0, weight)
        zero = jnp.zeros((8, n3), f32)
        x = b
        for _ in range(7):
            above = jnp.concatenate([zero, x[:-8]], axis=0)
            below = jnp.concatenate([x[8:], zero], axis=0)
            x = (0.2 * x + b + weight * (above + below)
                 + (left * pltpu.roll(x, 1, 1) + right * pltpu.roll(x, n3 - 1, 1)))
        mid = REACH * 8
        return [x[mid - 8:mid], x[mid:mid + 8], x[mid + 8:mid + 16]]

    def below(f, turn, first_gather):
        def change(r):
            dl[r] = relaxed0(f, r) - f[r]
        loop(4, 20, change)
        for i, x in enumerate(restrict(dl, 4, 8, ny)):
            b1[2 + i] = x * wide(ratio[0], n1) * s1[2 + i]
        for r in range(4, 8):
            u1[r] = relaxed(b1, b1, k1, r) - b1[r]
        bb = b2.at[turn]
        for i, x in enumerate(restrict(u1, 4, 2, n1)):
            bb[2 + i] = x * wide(ratio[1], n2) * s2[2 + i]
        swap(4 + turn, bb.at[2:4], bb.at[4:6], bb.at[2:4], bb.at[0:2])
        for r in range(2, 4):
            u2[r] = relaxed(bb, bb, k2, r) - bb[r]
        mine = restrict(u2, 2, 1, n2)[0] * ratio[2] * s3own[...]
        own = b3own.at[turn]
        own[...] = mine
        win[1 + turn, REACH] = mine
        gather_start(1 + turn, own)
        if first_gather:
            win[0, REACH] = s3own[...]
            gather_wait(0, s3own)
        gather_wait(1 + turn, own)
        f3 = coarse(1 + turn, win[0])
        for i, x in enumerate(prolong(f3)):
            for j in (0, 1):
                r = 2 * i + j
                u2[r] = bb[r] + s2[r] * x
        f2 = [relaxed(u2, bb, k2, r) for r in range(1, 5)]
        for i, x in enumerate(prolong(f2)):
            for j in (0, 1):
                r = 2 + 2 * i + j
                u1[r] = b1[r] + s1[r] * x
        for r in range(3, 9):
            v1[r] = relaxed(u1, b1, k1, r)
        for i, x in enumerate(prolong([v1[r] for r in range(3, 9)])):
            for j in (0, 1):
                r = 6 + 2 * i + j
                up[r] = f[r] + s0[r] * x

    def solve(which, out, finish):
        turn = 2 * which
        below(f0, turn, which == 0)
        second = f1.at[which]

        def first(r):
            second[r] = relaxed0(up, r)
        loop(8, 16, first)
        swap(1 + which, second.at[8:8 + HALO], second.at[16:16 + HALO],
             second.at[16 - HALO:16], second.at[8 - HALO:8])

        def again(r):
            it[r] = relaxed0(second, r)
        loop(3, 21, again)
        below(it, turn + 1, False)
        for r in range(8):
            x = relaxed0(up, r + 8)
            out[r] = x
            finish(r, x)

    def to_target(r, x):
        misfit = jnp.sum(x, axis=0, keepdims=True) / 8.0 - survey[0, r:r + 1, :]
        tgt[8 + r:9 + r, :] = survey[1, r:r + 1, :] * misfit / 8.0

    def to_gradient(r, x):
        g_out[r:r + 1, :] = strips[0, 8 + r:9 + r, :] * jnp.sum(
            wide(strength, ny) * x, axis=0, keepdims=True)

    coefficients(False)
    solve(0, c_out, to_target)
    swap(3, tgt.at[8:16], tgt.at[16:24], tgt.at[8:16], tgt.at[0:8])
    for r in range(24):
        f0[r] = s0[r] * wide(g0, ny) * jnp.broadcast_to(tgt[r:r + 1, :], (8, ny))
    coefficients(True)
    solve(1, a_out, to_gradient)


def on_device(n, season_ids, season_table, shelf_mask, codes, spawn, survey):
    onehot = season_ids[:, None] == jnp.arange(season_table.shape[1], dtype=jnp.int32)[None, :]
    picked = jnp.sum(jnp.where(onehot[None], season_table[:, None, :], 0.0), axis=2)
    m, d, u, v, a = 0.03 * picked[0], picked[1], 0.5 * picked[2], 0.5 * picked[3], picked[4]
    diag = [m + 4.0 * d + u + v] + [4.0 ** l * m + 4.0 * 2.0 ** l * d for l in (1, 2, 3)]
    w = [0.8 / x for x in diag]
    prm = jnp.stack([w[0], w[0] * d, w[0] * u, w[0] * v, a,
                     w[1] * 2.0 * d, w[2] * 4.0 * d, w[3] * 8.0 * d,
                     diag[0] / diag[1], diag[1] / diag[2], diag[2] / diag[3]])
    prm = jnp.broadcast_to(prm[:, :, None], prm.shape + (128,))
    rows, ny = shelf_mask.shape
    fine = pltpu.VMEM((24, 8, ny), f32)
    lvl1 = pltpu.VMEM((12, 8, ny // 2), f32)
    lvl2 = pltpu.VMEM((6, 8, ny // 4), f32)
    slots = 2 * REACH + 1
    vm = pl.BlockSpec(memory_space=pltpu.VMEM)
    c, adj, g = pl.pallas_call(
        functools.partial(kernel, n, ny),
        out_shape=(jax.ShapeDtypeStruct((rows, 8, ny), f32),
                   jax.ShapeDtypeStruct((rows, 8, ny), f32),
                   jax.ShapeDtypeStruct((rows, ny), f32)),
        in_specs=[vm] * 5,
        out_specs=(vm, vm, vm),
        scratch_shapes=[
            pltpu.VMEM((3, 24, ny), f32), pltpu.VMEM((24, ny), f32),
            fine, fine, fine, fine, fine, fine, fine, fine,
            pltpu.VMEM((2, 24, 8, ny), f32), fine, fine, fine,
            lvl1, lvl1, lvl1, lvl1, lvl1, lvl2, lvl2,
            pltpu.VMEM((4, 6, 8, ny // 4), f32), lvl2,
            pltpu.VMEM((8, ny // 8), f32), pltpu.VMEM((4, 8, ny // 8), f32),
            pltpu.VMEM((5, slots, 8, ny // 8), f32),
            pltpu.SemaphoreType.DMA((8, 2)), pltpu.SemaphoreType.DMA((8, 2)),
            pltpu.SemaphoreType.DMA((5, slots)), pltpu.SemaphoreType.DMA((5, slots)),
        ],
        compiler_params=pltpu.CompilerParams(
            collective_id=0, has_side_effects=True, vmem_limit_bytes=48 << 20),
        cost_estimate=pl.CostEstimate(flops=60_000_000, bytes_accessed=1_000_000, transcendentals=0),
    )(prm, shelf_mask, codes, spawn, survey)
    return jnp.transpose(c, (1, 0, 2)), jnp.transpose(adj, (1, 0, 2)), g


def solution(mesh):
    in_specs = (P("peel"), P(), P("tile", None), P("tile", None), P("tile", None),
                P("peel", "tile", None))
    out_specs = (P("peel", "tile", None), P("peel", "tile", None), P("tile", "peel"))
    return jax.shard_map(
        functools.partial(on_device, mesh.shape["tile"]), mesh=mesh,
        in_specs=in_specs, out_specs=out_specs, check_vma=False)
```

profile of v0, /device:TPU:0, one launch (start us, length us, event | category | flops | bytes accessed | tf_op | source)
XLA Modules:
  0.0 77.5 jit_solution(16430698561607676092)
XLA Ops:
  0.6 0.0 copy-start
  0.6 0.8 iota_compare_fusion
  1.4 0.8 select_reduce_fusion
  2.2 0.0 copy-start.1
  2.3 0.1 broadcast_in_dim.33.prm
  2.4 0.0 copy-done
  2.4 0.6 copy-done.1
  3.0 0.0 copy-start.2
  3.0 0.8 copy-done.2
  3.8 0.0 copy-start.3
  3.8 0.8 copy-done.3
  4.5 70.6 %shard_map.85 = (f32[8,8,1024]{2,1,0:T(8,128)S(1)}, f32[8,8,1024]{2,1,0:T(8,128)S(1)}, f32[8,1024]{1,0:T(8,128)S(1)}) custom-call(f32[11,8,128]{2,1,0:T(8,128)S(1)} %broadcast_in_dim.33.prm, s32[8,1024]{1,0:T(8,128)S(1)} %copy-done.1, s32[8,1024]{1,0:T(8,128)S(1)} %copy-done.2, f32[8,1024]{1,0:T(8,128)S(1)} %copy-done.3, f32[2,8,1024]{2,1,0:T(8,128)S(1)} %copy-done), custom_call_target="tpu_custom_call" | custom-call | flops 60000000 | bytes 1000000 | tf_op jit(solution)/shard_map/pallas_call | solution.py:289
  75.2 0.9 %copy.11 = f32[8,8,1024]{2,1,0:T(8,128)} copy(f32[8,8,1024]{2,0,1:T(8,128)S(1)} %bitcast.3) | data formatting | bytes 524288
  76.0 0.9 %copy.12 = f32[8,8,1024]{2,1,0:T(8,128)} copy(f32[8,8,1024]{2,0,1:T(8,128)S(1)} %bitcast.2) | data formatting | bytes 524288
  76.9 0.6 copy.14
  (6 shorter events, 0.1 us)
Async XLA Ops:
  0.6 1.8 %copy-start = (f32[2,8,1024]{2,1,0:T(8,128)S(1)}, f32[2,8,1024]{2,1,0:T(8,128)}, u32[]{:S(2)}) copy-start(f32[2,8,1024]{2,1,0:T(8,128)} %survey.1) | copy-start | bytes 196612
  2.2 0.8 copy-start.1
  3.0 0.8 copy-start.2
  3.8 0.8 copy-start.3
where the time goes:
time: 77.9 us; the launch traced here: 77.5 us
  Pallas kernels  70.6 us (91%)
  local copies, waits for them, and re-layouts  4.6 us (6%)
  other arithmetic  1.58 us (2%)
    pallas_call x1, Pallas kernels, on_device(): pl.pallas_call(functools.partial(kernel, n, ny), out_shape=(jax.ShapeDtyp...  70.6 us
    unnamed x11, local copies, waits for them, and re-layouts  4.48 us

commit v1 on v0

--- a/solution.py
+++ b/solution.py
@@ -11,14 +11,14 @@
 f32, bf16 = jnp.float32, jnp.bfloat16
 REACH = 8
 STRIP = 8
-HALO = 6
+HALO = 5
 
 
 def wide(p, width):
     return jnp.concatenate([p] * (width // 128), axis=1) if width > 128 else p
 
 
-def kernel(n, ny, prm, mask, codes, spawn, survey, c_out, a_out, g_out,
+def kernel(n, ny, ids, table, mask, codes, spawn, survey, c_out, a_out, g_out,
            strips, tgt, s0, west, south, f0, cn, cs, cw, ce, f1, it, up, dl,
            s1, k1, b1, u1, v1, s2, k2, b2, u2, s3own, b3own, win,
            send_n, recv_n, send_g, recv_g):
@@ -49,6 +49,8 @@
             src_ref=src, dst_ref=dst, send_sem=ssem, recv_sem=rsem,
             device_id={"tile": me + d}, device_id_type=pl.DeviceIdType.MESH)
 
+    pending = []
+
     def swap(k, up_src, up_dst, down_src, down_dst):
         def at(d):
             side = 0 if d < 0 else 1
@@ -56,25 +58,28 @@
             return copy(src, dst, send_n.at[k, side], recv_n.at[k, side], d)
         for d in (-1, 1):
             guarded(d, lambda d=d: at(d).start())
+            pending.append((d, lambda d=d: at(d).wait_send()))
+
+    def arrive(k, up_src, up_dst, down_src, down_dst):
         guarded(1, lambda: copy(up_src, up_dst, send_n.at[k, 0], recv_n.at[k, 0], 1).wait_recv())
         guarded(-1, lambda: copy(down_src, down_dst, send_n.at[k, 1], recv_n.at[k, 1], -1).wait_recv())
-        for d in (-1, 1):
-            guarded(d, lambda d=d: at(d).wait_send())
 
     def gather_start(k, src):
         for d in offsets:
             guarded(d, lambda d=d: copy(src, win.at[k, REACH - d], send_g.at[k, REACH - d],
                                         recv_g.at[k, REACH - d], d).start())
+            pending.append((d, lambda d=d: copy(
+                src, win.at[k, REACH - d], send_g.at[k, REACH - d],
+                recv_g.at[k, REACH - d], d).wait_send()))
 
     def gather_wait(k, src):
         for d in offsets:
             guarded(d, lambda d=d: copy(src, win.at[k, REACH + d], send_g.at[k, REACH + d],
                                         recv_g.at[k, REACH + d], d).wait_recv())
-        for d in offsets:
-            guarded(d, lambda d=d: copy(src, win.at[k, REACH - d], send_g.at[k, REACH - d],
-                                        recv_g.at[k, REACH - d], d).wait_send())
-
-    swap(0, strips.at[:, 8:16], strips.at[:, 16:24], strips.at[:, 8:16], strips.at[:, 0:8])
+
+    ends = (strips.at[:, 8:16], strips.at[:, 16:24], strips.at[:, 8:16], strips.at[:, 0:8])
+    swap(0, *ends)
+    arrive(0, *ends)
 
     gi = lax.broadcasted_iota(jnp.int32, (256, 128), 0)
     gj = lax.broadcasted_iota(jnp.int32, (256, 128), 1)
@@ -121,9 +126,19 @@
         return (jnp.where(lane == 0, 0.0, pltpu.roll(x, 1, 1)),
                 jnp.where(lane == width - 1, 0.0, pltpu.roll(x, width - 1, 1)))
 
-    g0, dd, uu, vv, strength = prm[0], prm[1], prm[2], prm[3], prm[4]
-    kappa = [None, prm[5], prm[6], prm[7]]
-    ratio = [prm[8], prm[9], prm[10]]
+    one = ids[...] == lax.broadcasted_iota(jnp.int32, (8, table.shape[1]), 1)
+
+    def pick(k):
+        x = jnp.sum(jnp.where(one, table[k:k + 1, :], 0.0), axis=1, keepdims=True)
+        return jnp.broadcast_to(x, (8, 128))
+    mort, diff, strength = 0.03 * pick(0), pick(1), pick(4)
+    u, v = 0.5 * pick(2), 0.5 * pick(3)
+    diag = [mort + 4.0 * diff + u + v]
+    diag += [4.0 ** l * mort + 4.0 * 2.0 ** l * diff for l in (1, 2, 3)]
+    w = [0.8 / x for x in diag]
+    g0, dd, uu, vv = w[0], w[0] * diff, w[0] * u, w[0] * v
+    kappa = [2.0 ** l * diff * w[l] for l in range(4)]
+    ratio = [diag[l] / diag[l + 1] for l in range(3)]
 
     for r in range(24):
         s0[r] = jnp.broadcast_to(strips[0, r:r + 1, :], (8, ny))
@@ -194,9 +209,6 @@
         return [x[mid - 8:mid], x[mid:mid + 8], x[mid + 8:mid + 16]]
 
     def below(f, turn, first_gather):
-        def change(r):
-            dl[r] = relaxed0(f, r) - f[r]
-        loop(4, 20, change)
         for i, x in enumerate(restrict(dl, 4, 8, ny)):
             b1[2 + i] = x * wide(ratio[0], n1) * s1[2 + i]
         for r in range(4, 8):
@@ -204,7 +216,9 @@
         bb = b2.at[turn]
         for i, x in enumerate(restrict(u1, 4, 2, n1)):
             bb[2 + i] = x * wide(ratio[1], n2) * s2[2 + i]
-        swap(4 + turn, bb.at[2:4], bb.at[4:6], bb.at[2:4], bb.at[0:2])
+        ends = (bb.at[2:4], bb.at[4:6], bb.at[2:4], bb.at[0:2])
+        swap(4 + turn, *ends)
+        arrive(4 + turn, *ends)
         for r in range(2, 4):
             u2[r] = relaxed(bb, bb, k2, r) - bb[r]
         mine = restrict(u2, 2, 1, n2)[0] * ratio[2] * s3own[...]
@@ -235,18 +249,31 @@
 
     def solve(which, out, finish):
         turn = 2 * which
+
+        def change(f, lo, hi):
+            def row(r):
+                dl[r] = relaxed0(f, r) - f[r]
+            loop(lo, hi, row)
+        change(f0, 4, 20)
         below(f0, turn, which == 0)
         second = f1.at[which]
 
         def first(r):
             second[r] = relaxed0(up, r)
-        loop(8, 16, first)
-        swap(1 + which, second.at[8:8 + HALO], second.at[16:16 + HALO],
-             second.at[16 - HALO:16], second.at[8 - HALO:8])
+        loop(7, 17, first)
+        ends = (second.at[9:9 + HALO], second.at[17:17 + HALO],
+                second.at[15 - HALO:15], second.at[7 - HALO:7])
+        swap(1 + which, *ends)
 
         def again(r):
             it[r] = relaxed0(second, r)
-        loop(3, 21, again)
+        loop(8, 16, again)
+        change(it, 9, 15)
+        arrive(1 + which, *ends)
+        loop(3, 8, again)
+        loop(16, 21, again)
+        change(it, 4, 9)
+        change(it, 15, 20)
         below(it, turn + 1, False)
         for r in range(8):
             x = relaxed0(up, r + 8)
@@ -263,23 +290,18 @@
 
     coefficients(False)
     solve(0, c_out, to_target)
-    swap(3, tgt.at[8:16], tgt.at[16:24], tgt.at[8:16], tgt.at[0:8])
+    ends = (tgt.at[8:16], tgt.at[16:24], tgt.at[8:16], tgt.at[0:8])
+    swap(3, *ends)
+    coefficients(True)
+    arrive(3, *ends)
     for r in range(24):
         f0[r] = s0[r] * wide(g0, ny) * jnp.broadcast_to(tgt[r:r + 1, :], (8, ny))
-    coefficients(True)
     solve(1, a_out, to_gradient)
+    for d, wait in pending:
+        guarded(d, wait)
 
 
 def on_device(n, season_ids, season_table, shelf_mask, codes, spawn, survey):
-    onehot = season_ids[:, None] == jnp.arange(season_table.shape[1], dtype=jnp.int32)[None, :]
-    picked = jnp.sum(jnp.where(onehot[None], season_table[:, None, :], 0.0), axis=2)
-    m, d, u, v, a = 0.03 * picked[0], picked[1], 0.5 * picked[2], 0.5 * picked[3], picked[4]
-    diag = [m + 4.0 * d + u + v] + [4.0 ** l * m + 4.0 * 2.0 ** l * d for l in (1, 2, 3)]
-    w = [0.8 / x for x in diag]
-    prm = jnp.stack([w[0], w[0] * d, w[0] * u, w[0] * v, a,
-                     w[1] * 2.0 * d, w[2] * 4.0 * d, w[3] * 8.0 * d,
-                     diag[0] / diag[1], diag[1] / diag[2], diag[2] / diag[3]])
-    prm = jnp.broadcast_to(prm[:, :, None], prm.shape + (128,))
     rows, ny = shelf_mask.shape
     fine = pltpu.VMEM((24, 8, ny), f32)
     lvl1 = pltpu.VMEM((12, 8, ny // 2), f32)
@@ -291,7 +313,7 @@
         out_shape=(jax.ShapeDtypeStruct((rows, 8, ny), f32),
                    jax.ShapeDtypeStruct((rows, 8, ny), f32),
                    jax.ShapeDtypeStruct((rows, ny), f32)),
-        in_specs=[vm] * 5,
+        in_specs=[vm] * 6,
         out_specs=(vm, vm, vm),
         scratch_shapes=[
             pltpu.VMEM((3, 24, ny), f32), pltpu.VMEM((24, ny), f32),
@@ -307,7 +329,7 @@
         compiler_params=pltpu.CompilerParams(
             collective_id=0, has_side_effects=True, vmem_limit_bytes=48 << 20),
         cost_estimate=pl.CostEstimate(flops=60_000_000, bytes_accessed=1_000_000, transcendentals=0),
-    )(prm, shelf_mask, codes, spawn, survey)
+    )(season_ids[:, None], season_table, shelf_mask, codes, spawn, survey)
     return jnp.transpose(c, (1, 0, 2)), jnp.transpose(adj, (1, 0, 2)), g
 
 

time: 77.9 us -> 72.6 us (0.932)
  Pallas kernels: 70.6 us -> 65.4 us
  other arithmetic: 1.58 us -> 0 us
  local copies, waits for them, and re-layouts: 4.6 us -> 6.18 us
    pallas_call x1, Pallas kernels: 70.6 us -> 65.4 us  [on_device(): pl.pallas_call(functools.partial(kernel, n, ny), out_shape=(jax.ShapeDtyp...]
    unnamed x11 -> x13, local copies, waits for them, and re-layouts: 4.48 us -> 5.45 us
where the time goes in v1:
time: 72.6 us; the launch traced here: 72.2 us
  Pallas kernels  65.4 us (90%)
  local copies, waits for them, and re-layouts  6.18 us (9%)
    pallas_call x1, Pallas kernels, on_device(): pl.pallas_call(functools.partial(kernel, n, ny), out_shape=(jax.ShapeDtyp...  65.4 us
    unnamed x13, local copies, waits for them, and re-layouts  5.45 us

profile of v1, /device:TPU:0, one launch (start us, length us, event | category | flops | bytes accessed | tf_op | source)
XLA Modules:
  0.0 72.2 jit_solution(1906666768017440623)
XLA Ops:
  0.6 0.0 copy-start.4
  0.6 0.7 %copy.9.ids = s32[8,1]{1,0:T(8,128)S(1)} copy(s32[8,1]{0,1:T(1,128)} %bitcast.5) | data formatting | bytes 64 | tf_op jit(solution)/shard_map/broadcast_in_dim | solution.py:332
  1.4 0.0 copy-done.4
  1.4 0.0 copy-start
  1.4 0.8 %copy-done = f32[2,8,1024]{2,1,0:T(8,128)S(1)} copy-done((f32[2,8,1024]{2,1,0:T(8,128)S(1)}, f32[2,8,1024]{2,1,0:T(8,128)}, u32[]{:S(2)}) %copy-start) | copy-done | bytes 65560
  2.2 0.0 copy-start.1
  2.2 0.8 %copy-done.1 = s32[8,1024]{1,0:T(8,128)S(1)} copy-done((s32[8,1024]{1,0:T(8,128)S(1)}, s32[8,1024]{1,0:T(8,128)}, u32[]{:S(2)}) %copy-start.1) | copy-done | bytes 32792
  3.0 0.0 copy-start.2
  3.0 0.8 %copy-done.2 = s32[8,1024]{1,0:T(8,128)S(1)} copy-done((s32[8,1024]{1,0:T(8,128)S(1)}, s32[8,1024]{1,0:T(8,128)}, u32[]{:S(2)}) %copy-start.2) | copy-done | bytes 32792
  3.7 0.0 copy-start.3
  3.7 0.8 %copy-done.3 = f32[8,1024]{1,0:T(8,128)S(1)} copy-done((f32[8,1024]{1,0:T(8,128)S(1)}, f32[8,1024]{1,0:T(8,128)}, u32[]{:S(2)}) %copy-start.3) | copy-done | bytes 32792
  4.5 65.4 %shard_map.85 = (f32[8,8,1024]{2,1,0:T(8,128)S(1)}, f32[8,8,1024]{2,1,0:T(8,128)S(1)}, f32[8,1024]{1,0:T(8,128)S(1)}) custom-call(s32[8,1]{1,0:T(8,128)S(1)} %copy.9.ids, f32[5,24]{1,0:T(8,128)S(1)} %copy-done.4, s32[8,1024]{1,0:T(8,128)S(1)} %copy-done.1, s32[8,1024]{1,0:T(8,128)S(1)} %copy-done.2, f32[8,1024]{1,0:T(8,128)S(1)} %copy-done.3, ...), custom_call_target="tpu_custom_call" | custom-call | flops 60000000 | bytes 1000000 | tf_op jit(solution)/shard_map/pallas_call | solution.py:311
  69.9 0.9 %copy.10 = f32[8,8,1024]{2,1,0:T(8,128)} copy(f32[8,8,1024]{2,0,1:T(8,128)S(1)} %bitcast.4) | data formatting | bytes 524288
  70.8 0.9 %copy.11 = f32[8,8,1024]{2,1,0:T(8,128)} copy(f32[8,8,1024]{2,0,1:T(8,128)S(1)} %bitcast.3) | data formatting | bytes 524288
  71.6 0.6 copy.13
Async XLA Ops:
  0.6 0.7 %copy-start.4 = (f32[5,24]{1,0:T(8,128)S(1)}, f32[5,24]{1,0:T(8,128)}, u32[]{:S(2)}) copy-start(f32[5,24]{1,0:T(8,128)} %table.1) | copy-start | bytes 1444
  1.4 0.8 %copy-start = (f32[2,8,1024]{2,1,0:T(8,128)S(1)}, f32[2,8,1024]{2,1,0:T(8,128)}, u32[]{:S(2)}) copy-start(f32[2,8,1024]{2,1,0:T(8,128)} %survey.1) | copy-start | bytes 196612
  2.2 0.8 %copy-start.1 = (s32[8,1024]{1,0:T(8,128)S(1)}, s32[8,1024]{1,0:T(8,128)}, u32[]{:S(2)}) copy-start(s32[8,1024]{1,0:T(8,128)} %mask.1) | copy-start | bytes 98308
  3.0 0.8 %copy-start.2 = (s32[8,1024]{1,0:T(8,128)S(1)}, s32[8,1024]{1,0:T(8,128)}, u32[]{:S(2)}) copy-start(s32[8,1024]{1,0:T(8,128)} %codes.1) | copy-start | bytes 98308
  3.7 0.8 %copy-start.3 = (f32[8,1024]{1,0:T(8,128)S(1)}, f32[8,1024]{1,0:T(8,128)}, u32[]{:S(2)}) copy-start(f32[8,1024]{1,0:T(8,128)} %spawn.1) | copy-start | bytes 98308

commit v2 on v1

--- a/solution.py
+++ b/solution.py
@@ -18,8 +18,8 @@
     return jnp.concatenate([p] * (width // 128), axis=1) if width > 128 else p
 
 
-def kernel(n, ny, ids, table, mask, codes, spawn, survey, c_out, a_out, g_out,
-           strips, tgt, s0, west, south, f0, cn, cs, cw, ce, f1, it, up, dl,
+def kernel(n, ny, ids, table, mask_in, codes_in, spawn_in, survey_in, c_out, a_out, g_out,
+           mask, codes, survey, load_sem, strips, tgt, s0, west, south, f0, cn, cs, cw, ce, f1, it, up, dl,
            s1, k1, b1, u1, v1, s2, k2, b2, u2, s3own, b3own, win,
            send_n, recv_n, send_g, recv_g):
     me = lax.axis_index("tile")
@@ -29,104 +29,50 @@
         ok = (me + d >= 0) & (me + d < n)
         pl.when(ok)(body)
 
-    strips[...] = jnp.zeros_like(strips)
+    loads = [pltpu.make_async_copy(src, dst, load_sem.at[k]) for k, (src, dst) in enumerate(
+        [(mask_in, mask), (codes_in, codes), (spawn_in, strips.at[2, 8:16]), (survey_in, survey)])]
+    for load in loads:
+        load.start()
+
+    for lo in (0, 16):
+        strips[:, lo:lo + 8, :] = jnp.zeros((3, 8, ny), f32)
     tgt[...] = jnp.zeros_like(tgt)
-    f1[...] = jnp.zeros_like(f1)
+    for k in (0, 1):
+        for lo in (0, 16):
+            f1[k, lo:lo + 8] = jnp.zeros((8, 8, ny), f32)
     b2[...] = jnp.zeros_like(b2)
     win[...] = jnp.zeros_like(win)
-    strips[0, STRIP:2 * STRIP, :] = jnp.where(mask[...] > 0, 1.0, 0.0).astype(f32)
-    strips[1, STRIP:2 * STRIP, :] = codes[...].astype(f32)
-    strips[2, STRIP:2 * STRIP, :] = spawn[...]
+    def loop(lo, hi, body):
+        step = next(k for k in (4, 5, 3, 2, 1) if (hi - lo) % k == 0)
+
+        def some(q, c):
+            for k in range(step):
+                body(lo + q * step + k)
+            return c
+        if hi - lo == step:
+            some(0, 0)
+        else:
+            lax.fori_loop(0, (hi - lo) // step, some, 0)
+
     barrier = pltpu.get_barrier_semaphore()
     offsets = [d for k in range(1, REACH + 1) for d in (-k, k)]
     for d in offsets:
         guarded(d, lambda d=d: pl.semaphore_signal(
             barrier, inc=1, device_id={"tile": me + d}, device_id_type=pl.DeviceIdType.MESH))
-    pl.semaphore_wait(barrier, jnp.minimum(me, REACH) + jnp.minimum(n - 1 - me, REACH))
-
-    def copy(src, dst, ssem, rsem, d):
-        return pltpu.make_async_remote_copy(
-            src_ref=src, dst_ref=dst, send_sem=ssem, recv_sem=rsem,
-            device_id={"tile": me + d}, device_id_type=pl.DeviceIdType.MESH)
-
-    pending = []
-
-    def swap(k, up_src, up_dst, down_src, down_dst):
-        def at(d):
-            side = 0 if d < 0 else 1
-            src, dst = (up_src, up_dst) if d < 0 else (down_src, down_dst)
-            return copy(src, dst, send_n.at[k, side], recv_n.at[k, side], d)
-        for d in (-1, 1):
-            guarded(d, lambda d=d: at(d).start())
-            pending.append((d, lambda d=d: at(d).wait_send()))
-
-    def arrive(k, up_src, up_dst, down_src, down_dst):
-        guarded(1, lambda: copy(up_src, up_dst, send_n.at[k, 0], recv_n.at[k, 0], 1).wait_recv())
-        guarded(-1, lambda: copy(down_src, down_dst, send_n.at[k, 1], recv_n.at[k, 1], -1).wait_recv())
-
-    def gather_start(k, src):
-        for d in offsets:
-            guarded(d, lambda d=d: copy(src, win.at[k, REACH - d], send_g.at[k, REACH - d],
-                                        recv_g.at[k, REACH - d], d).start())
-            pending.append((d, lambda d=d: copy(
-                src, win.at[k, REACH - d], send_g.at[k, REACH - d],
-                recv_g.at[k, REACH - d], d).wait_send()))
-
-    def gather_wait(k, src):
-        for d in offsets:
-            guarded(d, lambda d=d: copy(src, win.at[k, REACH + d], send_g.at[k, REACH + d],
-                                        recv_g.at[k, REACH + d], d).wait_recv())
-
-    ends = (strips.at[:, 8:16], strips.at[:, 16:24], strips.at[:, 8:16], strips.at[:, 0:8])
-    swap(0, *ends)
-    arrive(0, *ends)
-
-    gi = lax.broadcasted_iota(jnp.int32, (256, 128), 0)
-    gj = lax.broadcasted_iota(jnp.int32, (256, 128), 1)
-    pair_sum = jnp.where(gi // 2 == gj, 1.0, 0.0).astype(bf16)
-    hi_ = lax.broadcasted_iota(jnp.int32, (128, 256), 0)
-    hj_ = lax.broadcasted_iota(jnp.int32, (128, 256), 1)
-    spread = jnp.where(hj_ // 2 == hi_, 1.0, 0.0).astype(bf16)
-
-    def times(x, m):
-        big = x.astype(bf16)
-        rest = (x - big.astype(f32)).astype(bf16)
-        return (jnp.dot(big, m, preferred_element_type=f32)
-                + jnp.dot(rest, m, preferred_element_type=f32))
-
-    def restrict(src, lo, count, width):
-        blocks = width // 256
-        stack = []
-        for i in range(count):
-            x = src[lo + 2 * i] + src[lo + 2 * i + 1]
-            stack += [x[:, b * 256:(b + 1) * 256] for b in range(blocks)]
-        y = times(jnp.concatenate(stack, axis=0), pair_sum)
-        rows = []
-        for i in range(count):
-            parts = [y[(i * blocks + b) * 8:(i * blocks + b + 1) * 8] for b in range(blocks)]
-            rows.append(jnp.concatenate(parts, axis=1) if blocks > 1 else parts[0])
-        return rows
-
-    def prolong(rows):
-        blocks = rows[0].shape[1] // 128
-        stack = [x[:, b * 128:(b + 1) * 128] for x in rows for b in range(blocks)]
-        y = times(jnp.concatenate(stack, axis=0), spread)
-        out = []
-        for i in range(len(rows)):
-            parts = [y[(i * blocks + b) * 8:(i * blocks + b + 1) * 8] for b in range(blocks)]
-            out.append(jnp.concatenate(parts, axis=1) if blocks > 1 else parts[0])
-        return out
+    for load in loads[:3]:
+        load.wait()
+    strips[0, STRIP:2 * STRIP, :] = jnp.where(mask[...] > 0, 1.0, 0.0).astype(f32)
+    strips[1, STRIP:2 * STRIP, :] = codes[...].astype(f32)
 
     def lanes(width):
         return lax.broadcasted_iota(jnp.int32, (8, width), 1)
 
-    def shifted(x):
-        width = x.shape[1]
-        lane = lanes(width)
-        return (jnp.where(lane == 0, 0.0, pltpu.roll(x, 1, 1)),
-                jnp.where(lane == width - 1, 0.0, pltpu.roll(x, width - 1, 1)))
-
-    one = ids[...] == lax.broadcasted_iota(jnp.int32, (8, table.shape[1]), 1)
+    entries = lax.broadcasted_iota(jnp.int32, (8, table.shape[1]), 1)
+    season = lax.broadcasted_iota(jnp.int32, (8, table.shape[1]), 0)
+    wanted = jnp.full((8, table.shape[1]), ids[0], jnp.int32)
+    for k in range(1, 8):
+        wanted = jnp.where(season == k, ids[k], wanted)
+    one = wanted == entries
 
     def pick(k):
         x = jnp.sum(jnp.where(one, table[k:k + 1, :], 0.0), axis=1, keepdims=True)
@@ -140,27 +86,17 @@
     kappa = [2.0 ** l * diff * w[l] for l in range(4)]
     ratio = [diag[l] / diag[l + 1] for l in range(3)]
 
-    for r in range(24):
+    def spread_row(r):
         s0[r] = jnp.broadcast_to(strips[0, r:r + 1, :], (8, ny))
         code = strips[1, r:r + 1, :]
         top = jnp.where(code >= 2.0, 1.0, 0.0)
         west[r] = jnp.broadcast_to(1.0 - (code - 2.0 * top), (8, ny))
         south[r] = jnp.broadcast_to(1.0 - top, (8, ny))
         f0[r] = s0[r] * wide(g0 * strength, ny) * jnp.broadcast_to(strips[2, r:r + 1, :], (8, ny))
-    for i, x in enumerate(restrict(s0, 0, 12, ny)):
-        s1[i] = jnp.where(x > 0.0, 1.0, 0.0)
-        k1[i] = s1[i] * wide(kappa[1], n1)
-    for i, x in enumerate(restrict(s1, 0, 6, n1)):
-        s2[i] = jnp.where(x > 0.0, 1.0, 0.0)
-        k2[i] = s2[i] * wide(kappa[2], n2)
-    own3 = restrict(s2, 2, 1, n2)[0]
-    s3own[...] = jnp.where(own3 > 0.0, 1.0, 0.0)
-    gather_start(0, s3own)
-
-    def loop(lo, hi, body):
-        lax.fori_loop(lo, hi, lambda r, c: (body(r), c)[1], 0)
-
-    def coefficients(adjoint):
+    for r in range(8, 16):
+        spread_row(r)
+
+    def coefficients(adjoint, *ranges):
         D = wide(dd, ny)
         U = wide(uu, ny)
         V = wide(vv, ny)
@@ -179,7 +115,102 @@
             cs[r] = s * (D + U * as_)
             cw[r] = jnp.where(lane == 0, 0.0, s * (D + V * bw))
             ce[r] = jnp.where(lane == ny - 1, 0.0, s * (D + V * be))
-        loop(3, 21, row)
+        for lo, hi in ranges:
+            loop(lo, hi, row)
+
+    pl.semaphore_wait(barrier, jnp.minimum(me, REACH) + jnp.minimum(n - 1 - me, REACH))
+
+    def copy(src, dst, ssem, rsem, d):
+        return pltpu.make_async_remote_copy(
+            src_ref=src, dst_ref=dst, send_sem=ssem, recv_sem=rsem,
+            device_id={"tile": me + d}, device_id_type=pl.DeviceIdType.MESH)
+
+    pending = []
+
+    def swap(k, up_src, up_dst, down_src, down_dst):
+        def at(d):
+            side = 0 if d < 0 else 1
+            src, dst = (up_src, up_dst) if d < 0 else (down_src, down_dst)
+            return copy(src, dst, send_n.at[k, side], recv_n.at[k, side], d)
+        for d in (-1, 1):
+            guarded(d, lambda d=d: at(d).start())
+            pending.append((d, lambda d=d: at(d).wait_send()))
+
+    def arrive(k, up_src, up_dst, down_src, down_dst):
+        guarded(1, lambda: copy(up_src, up_dst, send_n.at[k, 0], recv_n.at[k, 0], 1).wait_recv())
+        guarded(-1, lambda: copy(down_src, down_dst, send_n.at[k, 1], recv_n.at[k, 1], -1).wait_recv())
+
+    def gather_start(k, src):
+        for d in offsets[::-1]:
+            guarded(d, lambda d=d: copy(src, win.at[k, REACH - d], send_g.at[k, REACH - d],
+                                        recv_g.at[k, REACH - d], d).start())
+            pending.append((d, lambda d=d: copy(
+                src, win.at[k, REACH - d], send_g.at[k, REACH - d],
+                recv_g.at[k, REACH - d], d).wait_send()))
+
+    def gather_wait(k, src):
+        for d in offsets:
+            guarded(d, lambda d=d: copy(src, win.at[k, REACH + d], send_g.at[k, REACH + d],
+                                        recv_g.at[k, REACH + d], d).wait_recv())
+
+    ends = (strips.at[:, 8:16], strips.at[:, 16:24], strips.at[:, 8:16], strips.at[:, 0:8])
+    swap(0, *ends)
+    coefficients(False, (8, 16))
+    arrive(0, *ends)
+    for r in (*range(8), *range(16, 24)):
+        spread_row(r)
+
+    gi = lax.broadcasted_iota(jnp.int32, (256, 128), 0)
+    gj = lax.broadcasted_iota(jnp.int32, (256, 128), 1)
+    pair_sum = jnp.where(gi // 2 == gj, 1.0, 0.0).astype(bf16)
+    hi_ = lax.broadcasted_iota(jnp.int32, (128, 256), 0)
+    hj_ = lax.broadcasted_iota(jnp.int32, (128, 256), 1)
+    spread = jnp.where(hj_ // 2 == hi_, 1.0, 0.0).astype(bf16)
+
+    def times(x, m):
+        big = x.astype(bf16)
+        rest = (x - big.astype(f32)).astype(bf16)
+        return (jnp.dot(big, m, preferred_element_type=f32)
+                + jnp.dot(rest, m, preferred_element_type=f32))
+
+    def restrict(src, lo, count, width):
+        blocks = width // 256
+        stack = []
+        for i in range(count):
+            x = src[lo + 2 * i] + src[lo + 2 * i + 1]
+            stack += [x[:, b * 256:(b + 1) * 256] for b in range(blocks)]
+        y = times(jnp.concatenate(stack, axis=0), pair_sum)
+        rows = []
+        for i in range(count):
+            parts = [y[(i * blocks + b) * 8:(i * blocks + b + 1) * 8] for b in range(blocks)]
+            rows.append(jnp.concatenate(parts, axis=1) if blocks > 1 else parts[0])
+        return rows
+
+    def prolong(rows):
+        blocks = rows[0].shape[1] // 128
+        stack = [x[:, b * 128:(b + 1) * 128] for x in rows for b in range(blocks)]
+        y = times(jnp.concatenate(stack, axis=0), spread)
+        out = []
+        for i in range(len(rows)):
+            parts = [y[(i * blocks + b) * 8:(i * blocks + b + 1) * 8] for b in range(blocks)]
+            out.append(jnp.concatenate(parts, axis=1) if blocks > 1 else parts[0])
+        return out
+
+    def shifted(x):
+        width = x.shape[1]
+        lane = lanes(width)
+        return (jnp.where(lane == 0, 0.0, pltpu.roll(x, 1, 1)),
+                jnp.where(lane == width - 1, 0.0, pltpu.roll(x, width - 1, 1)))
+
+    for i, x in enumerate(restrict(s0, 0, 12, ny)):
+        s1[i] = jnp.where(x > 0.0, 1.0, 0.0)
+        k1[i] = s1[i] * wide(kappa[1], n1)
+    for i, x in enumerate(restrict(s1, 0, 6, n1)):
+        s2[i] = jnp.where(x > 0.0, 1.0, 0.0)
+        k2[i] = s2[i] * wide(kappa[2], n2)
+    own3 = restrict(s2, 2, 1, n2)[0]
+    s3own[...] = jnp.where(own3 > 0.0, 1.0, 0.0)
+    gather_start(0, s3own)
 
     def relaxed0(f, r):
         x = f[r]
@@ -288,11 +319,12 @@
         g_out[r:r + 1, :] = strips[0, 8 + r:9 + r, :] * jnp.sum(
             wide(strength, ny) * x, axis=0, keepdims=True)
 
-    coefficients(False)
+    coefficients(False, (3, 8), (16, 21))
+    loads[3].wait()
     solve(0, c_out, to_target)
     ends = (tgt.at[8:16], tgt.at[16:24], tgt.at[8:16], tgt.at[0:8])
     swap(3, *ends)
-    coefficients(True)
+    coefficients(True, (3, 21))
     arrive(3, *ends)
     for r in range(24):
         f0[r] = s0[r] * wide(g0, ny) * jnp.broadcast_to(tgt[r:r + 1, :], (8, ny))
@@ -313,9 +345,11 @@
         out_shape=(jax.ShapeDtypeStruct((rows, 8, ny), f32),
                    jax.ShapeDtypeStruct((rows, 8, ny), f32),
                    jax.ShapeDtypeStruct((rows, ny), f32)),
-        in_specs=[vm] * 6,
+        in_specs=[pl.BlockSpec(memory_space=pltpu.SMEM), vm] + [pl.BlockSpec(memory_space=pltpu.HBM)] * 4,
         out_specs=(vm, vm, vm),
         scratch_shapes=[
+            pltpu.VMEM((rows, ny), jnp.int32), pltpu.VMEM((rows, ny), jnp.int32),
+            pltpu.VMEM((2, rows, ny), f32), pltpu.SemaphoreType.DMA((4,)),
             pltpu.VMEM((3, 24, ny), f32), pltpu.VMEM((24, ny), f32),
             fine, fine, fine, fine, fine, fine, fine, fine,
             pltpu.VMEM((2, 24, 8, ny), f32), fine, fine, fine,
@@ -329,7 +363,7 @@
         compiler_params=pltpu.CompilerParams(
             collective_id=0, has_side_effects=True, vmem_limit_bytes=48 << 20),
         cost_estimate=pl.CostEstimate(flops=60_000_000, bytes_accessed=1_000_000, transcendentals=0),
-    )(season_ids[:, None], season_table, shelf_mask, codes, spawn, survey)
+    )(season_ids, season_table, shelf_mask, codes, spawn, survey)
     return jnp.transpose(c, (1, 0, 2)), jnp.transpose(adj, (1, 0, 2)), g
 
 

time: 72.6 us -> 68.5 us (0.944)
  Pallas kernels: 65.4 us -> 60.6 us
    pallas_call x1, Pallas kernels: 65.4 us -> 60.6 us  [on_device(): pl.pallas_call(functools.partial(kernel, n, ny), out_shape=(jax.ShapeDtyp...]
    unnamed x13 -> x15, local copies, waits for them, and re-layouts: 5.45 us -> 6.78 us
    broadcast_in_dim x1 -> x0, local copies, waits for them, and re-layouts: 0.74 us -> none  [on_device(): season_ids[:, None]]
where the time goes in v2:
time: 68.5 us; the launch traced here: 68.1 us
  Pallas kernels  60.6 us (88%)
  local copies, waits for them, and re-layouts  6.78 us (10%)
    pallas_call x1, Pallas kernels, on_device(): pl.pallas_call(functools.partial(kernel, n, ny), out_shape=(jax.ShapeDtyp...  60.6 us
    unnamed x15, local copies, waits for them, and re-layouts  6.78 us

profile of v2, /device:TPU:0, one launch (start us, length us, event | category | flops | bytes accessed | tf_op | source)
XLA Modules:
  0.0 68.1 jit_solution(17443832616345761760)
XLA Ops:
  0.6 0.0 copy-start
  0.6 0.8 %copy-done = f32[2,8,1024]{2,1,0:T(8,128)S(1)} copy-done((f32[2,8,1024]{2,1,0:T(8,128)S(1)}, f32[2,8,1024]{2,1,0:T(8,128)}, u32[]{:S(2)}) %copy-start) | copy-done | bytes 65560
  1.5 0.0 copy-start.1
  1.5 0.8 %copy-done.1 = s32[8,1024]{1,0:T(8,128)S(1)} copy-done((s32[8,1024]{1,0:T(8,128)S(1)}, s32[8,1024]{1,0:T(8,128)}, u32[]{:S(2)}) %copy-start.1) | copy-done | bytes 32792
  2.2 0.0 copy-start.2
  2.2 0.8 %copy-done.2 = s32[8,1024]{1,0:T(8,128)S(1)} copy-done((s32[8,1024]{1,0:T(8,128)S(1)}, s32[8,1024]{1,0:T(8,128)}, u32[]{:S(2)}) %copy-start.2) | copy-done | bytes 32792
  3.0 0.0 copy-start.3
  3.0 0.8 %copy-done.3 = f32[8,1024]{1,0:T(8,128)S(1)} copy-done((f32[8,1024]{1,0:T(8,128)S(1)}, f32[8,1024]{1,0:T(8,128)}, u32[]{:S(2)}) %copy-start.3) | copy-done | bytes 32792
  3.7 0.0 copy-start.4
  3.8 0.7 %copy-done.4 = f32[5,24]{1,0:T(8,128)S(1)} copy-done((f32[5,24]{1,0:T(8,128)S(1)}, f32[5,24]{1,0:T(8,128)}, u32[]{:S(2)}) %copy-start.4) | copy-done | bytes 504
  4.4 0.0 copy-start.5
  4.4 0.7 copy-done.5
  5.1 60.6 %shard_map.85 = (f32[8,8,1024]{2,1,0:T(8,128)S(1)}, f32[8,8,1024]{2,1,0:T(8,128)S(1)}, f32[8,1024]{1,0:T(8,128)S(1)}) custom-call(s32[8]{0:T(128)S(1)} %copy-done.5, f32[5,24]{1,0:T(8,128)S(1)} %copy-done.4, s32[8,1024]{1,0:T(8,128)S(1)} %copy-done.1, s32[8,1024]{1,0:T(8,128)S(1)} %copy-done.2, f32[8,1024]{1,0:T(8,128)S(1)} %copy-done.3, ...), custom_call_target="tpu_custom_call" | custom-call | flops 60000000 | bytes 1000000 | tf_op jit(solution)/shard_map/pallas_call | solution.py:343
  65.7 0.9 %copy.9 = f32[8,8,1024]{2,1,0:T(8,128)} copy(f32[8,8,1024]{2,0,1:T(8,128)S(1)} %bitcast.3) | data formatting | bytes 524288
  66.6 0.9 %copy.10 = f32[8,8,1024]{2,1,0:T(8,128)} copy(f32[8,8,1024]{2,0,1:T(8,128)S(1)} %bitcast.2) | data formatting | bytes 524288
  67.5 0.6 copy.12
Async XLA Ops:
  0.6 0.8 %copy-start = (f32[2,8,1024]{2,1,0:T(8,128)S(1)}, f32[2,8,1024]{2,1,0:T(8,128)}, u32[]{:S(2)}) copy-start(f32[2,8,1024]{2,1,0:T(8,128)} %survey_in.1) | copy-start | bytes 196612
  1.5 0.8 %copy-start.1 = (s32[8,1024]{1,0:T(8,128)S(1)}, s32[8,1024]{1,0:T(8,128)}, u32[]{:S(2)}) copy-start(s32[8,1024]{1,0:T(8,128)} %mask_in.1) | copy-start | bytes 98308
  2.2 0.8 %copy-start.2 = (s32[8,1024]{1,0:T(8,128)S(1)}, s32[8,1024]{1,0:T(8,128)}, u32[]{:S(2)}) copy-start(s32[8,1024]{1,0:T(8,128)} %codes_in.1) | copy-start | bytes 98308
  3.0 0.8 %copy-start.3 = (f32[8,1024]{1,0:T(8,128)S(1)}, f32[8,1024]{1,0:T(8,128)}, u32[]{:S(2)}) copy-start(f32[8,1024]{1,0:T(8,128)} %spawn_in.1) | copy-start | bytes 98308
  3.7 0.7 %copy-start.4 = (f32[5,24]{1,0:T(8,128)S(1)}, f32[5,24]{1,0:T(8,128)}, u32[]{:S(2)}) copy-start(f32[5,24]{1,0:T(8,128)} %table.1) | copy-start | bytes 1444
  4.4 0.7 copy-start.5

commit v3 on v2

--- a/solution.py
+++ b/solution.py
@@ -9,7 +9,7 @@
 
 
 f32, bf16 = jnp.float32, jnp.bfloat16
-REACH = 8
+REACH = 9
 STRIP = 8
 HALO = 5
 
@@ -140,17 +140,20 @@
         guarded(1, lambda: copy(up_src, up_dst, send_n.at[k, 0], recv_n.at[k, 0], 1).wait_recv())
         guarded(-1, lambda: copy(down_src, down_dst, send_n.at[k, 1], recv_n.at[k, 1], -1).wait_recv())
 
+    def slot(k, i):
+        return win.at[0, i, 1] if k == 0 else win.at[k, i]
+
     def gather_start(k, src):
         for d in offsets[::-1]:
-            guarded(d, lambda d=d: copy(src, win.at[k, REACH - d], send_g.at[k, REACH - d],
+            guarded(d, lambda d=d: copy(src, slot(k, REACH - d), send_g.at[k, REACH - d],
                                         recv_g.at[k, REACH - d], d).start())
             pending.append((d, lambda d=d: copy(
-                src, win.at[k, REACH - d], send_g.at[k, REACH - d],
+                src, slot(k, REACH - d), send_g.at[k, REACH - d],
                 recv_g.at[k, REACH - d], d).wait_send()))
 
     def gather_wait(k, src):
         for d in offsets:
-            guarded(d, lambda d=d: copy(src, win.at[k, REACH + d], send_g.at[k, REACH + d],
+            guarded(d, lambda d=d: copy(src, slot(k, REACH + d), send_g.at[k, REACH + d],
                                         recv_g.at[k, REACH + d], d).wait_recv())
 
     ends = (strips.at[:, 8:16], strips.at[:, 16:24], strips.at[:, 8:16], strips.at[:, 0:8])
@@ -208,9 +211,9 @@
     for i, x in enumerate(restrict(s1, 0, 6, n1)):
         s2[i] = jnp.where(x > 0.0, 1.0, 0.0)
         k2[i] = s2[i] * wide(kappa[2], n2)
-    own3 = restrict(s2, 2, 1, n2)[0]
-    s3own[...] = jnp.where(own3 > 0.0, 1.0, 0.0)
-    gather_start(0, s3own)
+    for i, x in enumerate(restrict(s2, 0, 3, n2)):
+        s3own[i] = jnp.where(x > 0.0, 1.0, 0.0)
+    gather_start(0, s3own.at[1])
 
     def relaxed0(f, r):
         x = f[r]
@@ -222,10 +225,11 @@
         w, e = shifted(x)
         return 0.2 * x + b[r] + k[r] * ((f[r - 1] + f[r + 1]) + (w + e))
 
-    def coarse(k, s3):
-        src = win[k]
-        b = jnp.concatenate([src[i] for i in range(2 * REACH + 1)], axis=0)
-        weight = jnp.concatenate([s3[i] * kappa[3] for i in range(2 * REACH + 1)], axis=0)
+    def coarse(k):
+        inner = range(1, 2 * REACH)
+        b = jnp.concatenate([win[k, i, 1] + (win[k, i - 1, 2] + win[k, i + 1, 0])
+                             for i in inner], axis=0)
+        weight = jnp.concatenate([win[0, i, 1] * kappa[3] for i in inner], axis=0)
         lane = lax.broadcasted_iota(jnp.int32, b.shape, 1)
         left = jnp.where(lane == 0, 0.0, weight)
         right = jnp.where(lane == n3 - 1, 0.0, weight)
@@ -236,7 +240,7 @@
             below = jnp.concatenate([x[8:], zero], axis=0)
             x = (0.2 * x + b + weight * (above + below)
                  + (left * pltpu.roll(x, 1, 1) + right * pltpu.roll(x, n3 - 1, 1)))
-        mid = REACH * 8
+        mid = (REACH - 1) * 8
         return [x[mid - 8:mid], x[mid:mid + 8], x[mid + 8:mid + 16]]
 
     def below(f, turn, first_gather):
@@ -248,20 +252,28 @@
         for i, x in enumerate(restrict(u1, 4, 2, n1)):
             bb[2 + i] = x * wide(ratio[1], n2) * s2[2 + i]
         ends = (bb.at[2:4], bb.at[4:6], bb.at[2:4], bb.at[0:2])
+        for r in (2, 3):
+            x = bb[r]
+            w, e = shifted(x)
+            u2[r] = 0.2 * x + k2[r] * (bb[5 - r] + (w + e))
+        zero = jnp.zeros((8, n2), f32)
+        u2[0] = zero
+        u2[1] = k2[1] * bb[2]
+        u2[4] = k2[4] * bb[3]
+        u2[5] = zero
+        own = b3own.at[turn]
+        for i, x in enumerate(restrict(u2, 0, 3, n2)):
+            mine = x * ratio[2] * s3own[i]
+            own[i] = mine
+            win[1 + turn, REACH, i] = mine
+        gather_start(1 + turn, own)
         swap(4 + turn, *ends)
+        if first_gather:
+            win[0, REACH, 1] = s3own[1]
+            gather_wait(0, s3own.at[1])
+        gather_wait(1 + turn, own)
+        f3 = coarse(1 + turn)
         arrive(4 + turn, *ends)
-        for r in range(2, 4):
-            u2[r] = relaxed(bb, bb, k2, r) - bb[r]
-        mine = restrict(u2, 2, 1, n2)[0] * ratio[2] * s3own[...]
-        own = b3own.at[turn]
-        own[...] = mine
-        win[1 + turn, REACH] = mine
-        gather_start(1 + turn, own)
-        if first_gather:
-            win[0, REACH] = s3own[...]
-            gather_wait(0, s3own)
-        gather_wait(1 + turn, own)
-        f3 = coarse(1 + turn, win[0])
         for i, x in enumerate(prolong(f3)):
             for j in (0, 1):
                 r = 2 * i + j
@@ -355,8 +367,8 @@
             pltpu.VMEM((2, 24, 8, ny), f32), fine, fine, fine,
             lvl1, lvl1, lvl1, lvl1, lvl1, lvl2, lvl2,
             pltpu.VMEM((4, 6, 8, ny // 4), f32), lvl2,
-            pltpu.VMEM((8, ny // 8), f32), pltpu.VMEM((4, 8, ny // 8), f32),
-            pltpu.VMEM((5, slots, 8, ny // 8), f32),
+            pltpu.VMEM((3, 8, ny // 8), f32), pltpu.VMEM((4, 3, 8, ny // 8), f32),
+            pltpu.VMEM((5, slots, 3, 8, ny // 8), f32),
             pltpu.SemaphoreType.DMA((8, 2)), pltpu.SemaphoreType.DMA((8, 2)),
             pltpu.SemaphoreType.DMA((5, slots)), pltpu.SemaphoreType.DMA((5, slots)),
         ],

time: 68.5 us -> 63.3 us (0.924)
  Pallas kernels: 60.6 us -> 55.1 us
    pallas_call x1, Pallas kernels: 60.6 us -> 55.1 us  [on_device(): pl.pallas_call(functools.partial(kernel, n, ny), out_shape=(jax.ShapeDtyp...]
where the time goes in v3:
time: 63.3 us; the launch traced here: 62.5 us
  Pallas kernels  55.1 us (87%)
  local copies, waits for them, and re-layouts  6.78 us (11%)
  between operations  0.65 us (1%)
    pallas_call x1, Pallas kernels, on_device(): pl.pallas_call(functools.partial(kernel, n, ny), out_shape=(jax.ShapeDtyp...  55.1 us
    unnamed x15, local copies, waits for them, and re-layouts  6.78 us

profile of v3, /device:TPU:0, one launch (start us, length us, event | category | flops | bytes accessed | tf_op | source)
XLA Modules:
  0.0 62.5 jit_solution(13357394768941233827)
XLA Ops:
  0.6 0.0 copy-start
  0.6 0.8 %copy-done = f32[2,8,1024]{2,1,0:T(8,128)S(1)} copy-done((f32[2,8,1024]{2,1,0:T(8,128)S(1)}, f32[2,8,1024]{2,1,0:T(8,128)}, u32[]{:S(2)}) %copy-start) | copy-done | bytes 65560
  1.5 0.0 copy-start.1
  1.5 0.8 %copy-done.1 = s32[8,1024]{1,0:T(8,128)S(1)} copy-done((s32[8,1024]{1,0:T(8,128)S(1)}, s32[8,1024]{1,0:T(8,128)}, u32[]{:S(2)}) %copy-start.1) | copy-done | bytes 32792
  2.2 0.0 copy-start.2
  2.2 0.8 %copy-done.2 = s32[8,1024]{1,0:T(8,128)S(1)} copy-done((s32[8,1024]{1,0:T(8,128)S(1)}, s32[8,1024]{1,0:T(8,128)}, u32[]{:S(2)}) %copy-start.2) | copy-done | bytes 32792
  3.0 0.0 copy-start.3
  3.0 0.8 %copy-done.3 = f32[8,1024]{1,0:T(8,128)S(1)} copy-done((f32[8,1024]{1,0:T(8,128)S(1)}, f32[8,1024]{1,0:T(8,128)}, u32[]{:S(2)}) %copy-start.3) | copy-done | bytes 32792
  3.7 0.0 copy-start.4
  3.8 0.7 %copy-done.4 = f32[5,24]{1,0:T(8,128)S(1)} copy-done((f32[5,24]{1,0:T(8,128)S(1)}, f32[5,24]{1,0:T(8,128)}, u32[]{:S(2)}) %copy-start.4) | copy-done | bytes 504
  4.4 0.0 copy-start.5
  4.4 0.7 %copy-done.5 = s32[8]{0:T(128)S(1)} copy-done((s32[8]{0:T(128)S(1)}, s32[8]{0:T(128)}, u32[]{:S(2)}) %copy-start.5) | copy-done | bytes 56
  5.1 55.1 %shard_map.85 = (f32[8,8,1024]{2,1,0:T(8,128)S(1)}, f32[8,8,1024]{2,1,0:T(8,128)S(1)}, f32[8,1024]{1,0:T(8,128)S(1)}) custom-call(s32[8]{0:T(128)S(1)} %copy-done.5, f32[5,24]{1,0:T(8,128)S(1)} %copy-done.4, s32[8,1024]{1,0:T(8,128)S(1)} %copy-done.1, s32[8,1024]{1,0:T(8,128)S(1)} %copy-done.2, f32[8,1024]{1,0:T(8,128)S(1)} %copy-done.3, ...), custom_call_target="tpu_custom_call" | custom-call | flops 60000000 | bytes 1000000 | tf_op jit(solution)/shard_map/pallas_call | solution.py:355
  60.2 0.9 %copy.9 = f32[8,8,1024]{2,1,0:T(8,128)} copy(f32[8,8,1024]{2,0,1:T(8,128)S(1)} %bitcast.3) | data formatting | bytes 524288
  61.0 0.9 %copy.10 = f32[8,8,1024]{2,1,0:T(8,128)} copy(f32[8,8,1024]{2,0,1:T(8,128)S(1)} %bitcast.2) | data formatting | bytes 524288
  61.9 0.6 copy.12
Async XLA Ops:
  0.6 0.8 %copy-start = (f32[2,8,1024]{2,1,0:T(8,128)S(1)}, f32[2,8,1024]{2,1,0:T(8,128)}, u32[]{:S(2)}) copy-start(f32[2,8,1024]{2,1,0:T(8,128)} %survey_in.1) | copy-start | bytes 196612
  1.5 0.8 %copy-start.1 = (s32[8,1024]{1,0:T(8,128)S(1)}, s32[8,1024]{1,0:T(8,128)}, u32[]{:S(2)}) copy-start(s32[8,1024]{1,0:T(8,128)} %mask_in.1) | copy-start | bytes 98308
  2.2 0.8 %copy-start.2 = (s32[8,1024]{1,0:T(8,128)S(1)}, s32[8,1024]{1,0:T(8,128)}, u32[]{:S(2)}) copy-start(s32[8,1024]{1,0:T(8,128)} %codes_in.1) | copy-start | bytes 98308
  3.0 0.8 %copy-start.3 = (f32[8,1024]{1,0:T(8,128)S(1)}, f32[8,1024]{1,0:T(8,128)}, u32[]{:S(2)}) copy-start(f32[8,1024]{1,0:T(8,128)} %spawn_in.1) | copy-start | bytes 98308
  3.7 0.7 %copy-start.4 = (f32[5,24]{1,0:T(8,128)S(1)}, f32[5,24]{1,0:T(8,128)}, u32[]{:S(2)}) copy-start(f32[5,24]{1,0:T(8,128)} %table.1) | copy-start | bytes 1444
  4.4 0.7 %copy-start.5 = (s32[8]{0:T(128)S(1)}, s32[8]{0:T(128)}, u32[]{:S(2)}) copy-start(s32[8]{0:T(128)} %ids.1) | copy-start | bytes 100
